TPU v7x, 32 devices: a whole 2x2x4 slice. The times are simulated.
32 devices in a mesh: ctx: 8 (over z, y), tp: 4 (over x, core).
Axes of the slice: x: 2, y: 2, z: 4, core: 2. Of those that a mesh axis runs over, the one named last changes fastest.
Arguments:
- features: bfloat16 [1024, 3, 4096], P('ctx', None, 'tp'), may hold values from -6 to 6
- short_taps: float32 [3, 3, 4096], P(None, None, 'tp'), may hold values from -3 to 3
- residues: float32 [16, 4096], P(None, 'tp'), may hold values from -2 to 2
- log_rate: float32 [16, 4096], P(None, 'tp'), may hold values from -13 to -3.5, as said below
- out_weight: bfloat16 [4096, 8192], P('tp'), may hold values from -0.09375 to 0.09375
- grad_out: bfloat16 [1024, 8192], P('ctx', 'tp'), may hold values from -6 to 6
Outputs:
- grad_features: bfloat16 [1024, 3, 4096], P('ctx', None, 'tp')
- grad_taps: float32 [3, 3, 4096], P(None, None, 'tp')
- grad_residues: float32 [16, 4096], P(None, 'tp')
- grad_log_rate: float32 [16, 4096], P(None, 'tp')
- grad_weight_t: float32 [8192, 4096], P('ctx', 'tp')
Inputs may be any that keep to these rules, and one draw needn't show every extreme that they name: `log_rate`: log of a decay rate per token.
All inputs are finite; a program needn't handle non-finite values.
Results may differ from a plain program's by a relative error of at most 0.0058.
Values may be sent and summed in bfloat16 or wider, within the bound.
A program may use at most 192 MiB of HBM per device.

v0:
```python
import jax
import jax.numpy as jnp
from jax import lax
from jax.sharding import PartitionSpec as P


def shifted(value, axis, steps):
    count = lax.axis_size(axis)
    first, last = (max(0, -steps), min(count, count - steps))
    return lax.ppermute(value, axis, [(source, source + steps) for source in range(first, last)])


def block_tables(residues, log_rate, block_len):
    decay_rate = jnp.exp(log_rate)
    amplitude = residues * jnp.exp(0.5 * log_rate)
    lag_steps = jnp.arange(block_len).astype(jnp.float32)
    kernel = jnp.sum(
        amplitude[:, None, :] * jnp.exp(-decay_rate[:, None, :] * lag_steps[None, :, None]), axis=0
    )
    row_ids = jnp.arange(block_len)[:, None]
    col_ids = jnp.arange(block_len)[None, :]
    distance = row_ids - col_ids
    toeplitz = jnp.where((distance >= 0)[:, :, None], kernel[jnp.maximum(distance, 0)], 0.0)
    injection = jnp.exp(-decay_rate[:, None, :] * (block_len - 1 - lag_steps)[None, :, None])
    readout = amplitude[:, None, :] * jnp.exp(
        -decay_rate[:, None, :] * (lag_steps + 1.0)[None, :, None]
    )
    return (decay_rate, toeplitz, injection, readout)


def combine_states(earlier, later):
    return (earlier[0] * later[0], later[0] * earlier[1] + later[1])


def long_conv(product, residues, log_rate):
    block_len = 128
    length, channels = product.shape
    block_count = length // block_len
    decay_rate, toeplitz, injection, readout = block_tables(residues, log_rate, block_len)
    blocks = product.reshape(block_count, block_len, channels)
    inside = jnp.einsum("ijc,bjc->bic", toeplitz, blocks, precision=lax.Precision.HIGHEST)
    entering = jnp.einsum("rjc,bjc->brc", injection, blocks, precision=lax.Precision.HIGHEST)
    carry_decay = jnp.broadcast_to(jnp.exp(-decay_rate * block_len), entering.shape)
    unused, states = lax.associative_scan(combine_states, (carry_decay, entering), axis=0)
    before = jnp.concatenate([jnp.zeros_like(states[:1]), states[:-1]], axis=0)
    from_past = jnp.einsum("ric,brc->bic", readout, before, precision=lax.Precision.HIGHEST)
    return (inside + from_past).reshape(length, channels)


def to_channels(values):
    return lax.all_to_all(values, "ctx", split_axis=1, concat_axis=0, tiled=True)


def to_tokens(values):
    return lax.all_to_all(values, "ctx", split_axis=0, concat_axis=1, tiled=True)


def per_device(features, short_taps, residues, log_rate, out_weight, grad_out):
    length = features.shape[0]
    tap_count = short_taps.shape[0]
    groups = lax.axis_size("ctx")
    position = lax.axis_index("ctx")
    rim_rows = shifted(features[length - (tap_count - 1) :], "ctx", 1)
    padded_in = jnp.concatenate([rim_rows, features], axis=0).astype(jnp.float32)
    shortened = sum(
        (
            short_taps[lag] * padded_in[tap_count - 1 - lag : tap_count - 1 - lag + length]
            for lag in range(tap_count)
        )
    )
    product = (shortened[:, 1] * shortened[:, 2]).astype(jnp.bfloat16)
    chan_width = product.shape[1] // groups
    local_residues = lax.dynamic_slice_in_dim(residues, position * chan_width, chan_width, 1)
    local_rates = lax.dynamic_slice_in_dim(log_rate, position * chan_width, chan_width, 1)
    product_chan = to_channels(product).astype(jnp.float32)
    conv_chan, pullback = jax.vjp(long_conv, product_chan, local_residues, local_rates)
    convolved = to_tokens(conv_chan.astype(jnp.bfloat16)).astype(jnp.float32)
    gated = (shortened[:, 0] * convolved).astype(jnp.bfloat16)
    cotangent = lax.all_gather(grad_out, "tp", axis=1, tiled=True)
    grad_weight_t = lax.psum_scatter(
        lax.dot_general(
            cotangent, gated, (((0,), (0,)), ((), ())), preferred_element_type=jnp.float32
        ),
        "ctx",
        scatter_dimension=0,
        tiled=True,
    )
    grad_gated = lax.dot_general(
        cotangent, out_weight, (((1,), (1,)), ((), ())), preferred_element_type=jnp.float32
    )
    grad_conv = (grad_gated * shortened[:, 0]).astype(jnp.bfloat16)
    grad_prod_chan, grad_res_local, grad_rate_local = pullback(
        to_channels(grad_conv).astype(jnp.float32)
    )
    grad_product = to_tokens(grad_prod_chan.astype(jnp.bfloat16)).astype(jnp.float32)
    grad_residues, grad_log_rate = (
        lax.all_gather(grad_res_local, "ctx", axis=1, tiled=True),
        lax.all_gather(grad_rate_local, "ctx", axis=1, tiled=True),
    )
    grad_short = jnp.stack(
        [grad_gated * convolved, grad_product * shortened[:, 2], grad_product * shortened[:, 1]],
        axis=1,
    )
    tail_rows = shifted(grad_short[: tap_count - 1], "ctx", -1)
    tail_pad = jnp.concatenate([grad_short, tail_rows], axis=0)
    grad_features = sum(
        (short_taps[lag] * tail_pad[lag : lag + length] for lag in range(tap_count))
    )
    partial_taps = jnp.stack(
        [
            jnp.sum(
                grad_short * padded_in[tap_count - 1 - lag : tap_count - 1 - lag + length], axis=0
            )
            for lag in range(tap_count)
        ],
        axis=0,
    )
    grad_taps = lax.psum(partial_taps, "ctx")
    return (
        grad_features.astype(jnp.bfloat16),
        grad_taps,
        grad_residues,
        grad_log_rate,
        grad_weight_t,
    )


def solution(mesh):
    return jax.shard_map(
        per_device,
        mesh=mesh,
        in_specs=(
            P("ctx", None, "tp"),
            P(None, None, "tp"),
            P(None, "tp"),
            P(None, "tp"),
            P("tp", None),
            P("ctx", "tp"),
        ),
        out_specs=(
            P("ctx", None, "tp"),
            P(None, None, "tp"),
            P(None, "tp"),
            P(None, "tp"),
            P("ctx", "tp"),
        ),
        check_vma=False,
    )
```

profile of v0, /device:TPU:0, one launch (start us, length us, event | category | flops | bytes accessed | tf_op | source)
XLA Modules:
  0.0 879.5 jit_solution(6375209423134570061)
XLA Ops:
  8.7 4.9 collective-permute-start
  20.7 5.3 all-to-all-start
  28.0 6.5 all-to-all-done
  38.6 13.0 %multiply_convert_fusion.1 = (bf16[128,1024]{1,0:T(8,128)(2,1)}, f32[128,1024]{1,0:T(8,128)}) fusion(f32[128,3,1024]{2,0,1:T(8,128)S(1)} %multiply_add_fusion, bf16[128,8192]{1,0:T(8,128)(2,1)} %all-gather.2.cloned.1.call-done, bf16[1024,8192]{1,0:T(8,128)(2,1)} %param.10), kind=kOutput, calls=%fused_computation.43 | convolution fusion | flops 2147745792 | bytes 20185088 | tf_op jit(solution)/shard_map/dot_general | solution.py:88
  53.4 4.1 all-to-all-start.2
  77.0 3.3 fusion.13
  80.3 5.6 select_bitcast_fusion
  85.9 9.3 %copy.155 = f32[128,128,128]{2,1,0:T(8,128)} copy(f32[128,128,128]{1,0,2:T(8,128)} %select_bitcast_fusion) | data formatting | bytes 16777216 | tf_op jit(solution)/shard_map/transpose(jvp(jit(_where)))/select_n | solution.py:23
  95.2 98.8 %scatter_custom_fusion = f32[128,128]{1,0:T(8,128)S(1)} fusion(s32[16384]{0:T(1024)} %maximum_bitcast_fusion, f32[16384,128]{1,0:T(8,128)} %bitcast.83, f32[]{:T(128)} %constant.7.clone.1), kind=kCustom, calls=%fused_computation.85 | custom fusion | flops 2097152 | bytes 66048 | tf_op jit(solution)/shard_map/transpose(jvp())/scatter-add | solution.py:23
  194.8 4.6 multiply_reduce_fusion.4
  200.3 54.8 %gather_fusion = f32[16384,128]{1,0:T(8,128)} fusion(f32[128,128]{1,0:T(8,128)S(1)} %copy.124, s32[16384]{0:T(1024)S(1)} %broadcast_clamp_fusion), kind=kCustom, calls=%fused_computation | custom fusion | bytes 16842752 | tf_op jit(solution)/shard_map/jvp()/gather | solution.py:23
  255.1 9.9 %broadcast_select_fusion = f32[128,128,128]{2,1,0:T(8,128)} fusion(f32[128,128,128]{2,1,0:T(8,128)} %bitcast.82, pred[128,128]{1,0:T(8,128)(4,1)} %subtract_compare_fusion), kind=kLoop, calls=%fused_computation.4 | loop fusion | flops 2097152 | bytes 16793600 | tf_op jit(solution)/shard_map/jvp(jit(_where))/select_n | solution.py:23
  265.1 9.3 %copy.126 = f32[128,128,128]{1,0,2:T(8,128)} copy(f32[128,128,128]{2,1,0:T(8,128)} %broadcast_select_fusion) | data formatting | bytes 16777216 | tf_op jit(solution)/shard_map/jvp(jit(_where))/select_n | solution.py:23
  274.3 10.1 %fusion.9 = bf16[8,128,128]{1,0,2:T(8,128)(2,1)S(1)} fusion(f32[128,8,128]{2,1,0:T(8,128)} %fusion.13, f32[128,128,128]{1,0,2:T(8,128)} %copy.126, bf16[128,8,128]{0,2,1:T(8,128)(2,1)} %all-to-all-done), kind=kOutput, calls=%fused_computation.26 | convolution fusion | flops 201588736 | bytes 9437184 | tf_op jit(solution)/shard_map/jvp(ijc,bjc->bic)/dot_general | solution.py:41
  284.5 12.0 %all_to_all.43 = bf16[8,128,128]{1,2,0:T(8,128)(2,1)S(1)} all-to-all(bf16[8,128,128]{1,2,0:T(8,128)(2,1)S(1)} %copy.130), channel_id=1, replica_groups=mesh['ctx'=8,'tp'=4] {'ctx'}, dimensions={0} | all-to-all | bytes 524288 | tf_op jit(solution)/shard_map/all_to_all | solution.py:55
  299.4 17.4 %convolution_bitcast_fusion = f32[8192,1024]{0,1:T(8,128)} fusion(bf16[128,8192]{1,0:T(8,128)(2,1)} %all-gather.2.cloned.1.call-done, f32[128,1024]{1,0:T(8,128)} %copy.152, f32[128,3,1024]{2,0,1:T(8,128)S(1)} %multiply_add_fusion), kind=kOutput, calls=%fused_computation.2 | convolution fusion | flops 2147745792 | bytes 36700160 | tf_op jit(solution)/shard_map/dot_general | solution.py:81
  330.5 7.5 fusion.8
  338.7 4.1 all-to-all-start.3
  342.8 3.3 fusion.5
  351.6 32.6 %all_gather.11 = f32[16,1024]{1,0:T(8,128)S(1)} all-gather(f32[16,128]{1,0:T(8,128)S(1)} %get-tuple-element.56), channel_id=1, replica_groups=mesh['ctx'=8,'tp'=4] {'ctx'}, dimensions={1}, use_global_device_ids=true | all-gather | bytes 73728 | tf_op jit(solution)/shard_map/all_gather | solution.py:98
  391.0 32.0 %all_gather.10 = f32[16,1024]{1,0:T(8,128)S(1)} all-gather(f32[16,128]{1,0:T(8,128)S(1)} %get-tuple-element.57), channel_id=1, replica_groups=mesh['ctx'=8,'tp'=4] {'ctx'}, dimensions={1}, use_global_device_ids=true | all-gather | bytes 73728 | tf_op jit(solution)/shard_map/all_gather | solution.py:97
  425.1 40.6 %psum.7 = f32[3,3,1024]{2,1,0:T(4,128)} all-reduce(f32[3,3,1024]{2,1,0:T(4,128)S(1)} %pad_maximum_fusion.2), channel_id=1, replica_groups=mesh['ctx'=8,'tp'=4] {'ctx'}, use_global_device_ids=true, to_apply=%region_4.5 | all-reduce | flops 9216 | bytes 73728 | tf_op jit(solution)/shard_map/psum | solution.py:118
  465.8 400.1 %reduce-scatter.2.cloned.1.call-done = f32[1024,1024]{0,1:T(8,128)} async-done(((f32[8192,1024]{0,1:T(8,128)}), f32[1024,1024]{0,1:T(8,128)}) %reduce-scatter.2.cloned.1.call-update) | async-done | bytes 4194320 | tf_op jit(solution)/shard_map/reduce_scatter | solution.py:80
  865.8 5.3 copy.150
  (143 shorter events, 70.3 us)
Async XLA Ops:
  7.2 31.5 %all-gather.2.cloned.1.call-start = ((), (), s32[]{:S(2)}) async-start(), calls=%async_computation.5 | async-start | bytes 2621440 | tf_op jit(solution)/shard_map/all_gather | solution.py:79
  8.7 7.6 collective-permute-start
  13.6 20.9 %copy-start.20 = (f32[128]{0:T(128)}, f32[128]{0:T(128)S(1)}, u32[]{:S(2)}) copy-start(f32[128]{0:T(128)S(1)} %broadcast_subtract_fusion) | copy-start | bytes 1540
  15.0 23.6 %copy-start.15 = (f32[16,128]{1,0:T(8,128)}, f32[16,128]{1,0:T(8,128)S(1)}, u32[]{:S(2)}) copy-start(f32[16,128]{1,0:T(8,128)S(1)} %get-tuple-element.51) | copy-start | bytes 24580
  15.8 2.4 copy-start.3
  15.8 2.4 copy-start.5
  15.8 2.4 copy-start.7
  20.7 13.8 %all-to-all-start = ((bf16[128,8,128]{0,2,1:T(8,128)(2,1)}), bf16[128,8,128]{0,2,1:T(8,128)(2,1)}, u32[]{:S(2)}, u32[]{:S(2)}) async-start(bf16[128,8,128]{0,2,1:T(8,128)(2,1)} %bitcast.87), calls=%async_computation | async-start | bytes 524288 | tf_op jit(solution)/shard_map/all_to_all | solution.py:51
  38.6 19.2 %copy-start.17 = (f32[2,16,128]{2,1,0:T(8,128)}, f32[2,16,128]{2,1,0:T(8,128)S(1)}, u32[]{:S(2)}) copy-start(f32[2,16,128]{2,1,0:T(8,128)S(1)} %slice_add_fusion.3) | copy-start | bytes 49156
  53.4 12.3 %all-to-all-start.2 = ((bf16[128,8,128]{0,2,1:T(8,128)(2,1)}), bf16[128,8,128]{0,2,1:T(8,128)(2,1)}, u32[]{:S(2)}, u32[]{:S(2)}) async-start(bf16[128,8,128]{0,2,1:T(8,128)(2,1)} %bitcast.86), calls=%async_computation.2 | async-start | bytes 524288 | tf_op jit(solution)/shard_map/all_to_all | solution.py:51
  57.5 808.4 %reduce-scatter.2.cloned.1.call-start = ((), (), s32[]{:S(2)}) async-start(), calls=%async_computation.6 | async-start | bytes 37748736 | tf_op jit(solution)/shard_map/reduce_scatter | solution.py:80
  71.4 2.0 copy-start.10
  77.0 3.3 copy-start.2
  316.8 2.0 copy-start.18
  316.8 2.0 copy-start.16
  316.8 2.0 copy-start.22
  330.5 12.3 %copy-start.21 = (f32[128]{0:T(128)S(1)}, f32[128]{0:T(128)}, u32[]{:S(2)}) copy-start(f32[128]{0:T(128)} %copy-done.20) | copy-start | bytes 1540
  338.0 8.2 copy-start.19
  338.0 8.2 copy-start.9
  338.7 45.5 %all-to-all-start.3 = ((bf16[8,128,128]{1,2,0:T(8,128)(2,1)}), bf16[8,128,128]{1,2,0:T(8,128)(2,1)}, u32[]{:S(2)}, u32[]{:S(2)}) async-start(bf16[8,128,128]{1,2,0:T(8,128)(2,1)} %copy.137), calls=%async_computation.3 | async-start | bytes 524288 | tf_op jit(solution)/shard_map/all_to_all | solution.py:55
  389.6 33.3 %collective-permute-start.1 = (f32[2,3,1024]{2,0,1:T(2,128)S(1)}, f32[2,3,1024]{2,0,1:T(2,128)S(1)}, u32[]{:S(2)}, u32[]{:S(2)}) collective-permute-start(f32[2,3,1024]{2,0,1:T(2,128)S(1)} %slice.179), channel_id=1, source_target_pairs={{4,0},{8,4},{12,8},{16,12},{20,16},{24,20},{28,24},{5,1},{9,5},{13... | collective-permute-start | bytes 73736 | tf_op jit(solution)/shard_map/ppermute | solution.py:10
  390.9 32.3 %copy-start.4 = (f32[3,1024]{1,0:T(4,128)S(1)}, f32[3,1024]{1,0:T(4,128)}, u32[]{:S(2)}) copy-start(f32[3,1024]{1,0:T(4,128)} %copy-done.3) | copy-start | bytes 36868
  390.9 32.3 %copy-start.6 = (f32[3,1024]{1,0:T(4,128)S(1)}, f32[3,1024]{1,0:T(4,128)}, u32[]{:S(2)}) copy-start(f32[3,1024]{1,0:T(4,128)} %copy-done.5) | copy-start | bytes 36868
  390.9 32.3 %copy-start.8 = (f32[3,1024]{1,0:T(4,128)S(1)}, f32[3,1024]{1,0:T(4,128)}, u32[]{:S(2)}) copy-start(f32[3,1024]{1,0:T(4,128)} %copy-done.7) | copy-start | bytes 36868
  (6 other events, 6.9 us)
Sparse Core Ops, SparseCore 0:
  9.6 25.2 all-gather.1
  317.0 548.8 reduce-scatter.1
where the time goes:
time: 888 us; the launch traced here: 879 us
  waiting for transfers between devices  409 us (46%)
  other arithmetic  129 us (15%)
  blocking collectives  117 us (13%)
  local copies, waits for them, and re-layouts  116 us (13%)
  matrix products  72.8 us (8%)
  starting transfers between devices  20 us (2%)
  between operations  14.8 us (2%)
    reduce_scatter x1, waiting for transfers between devices, per_device(): lax.psum_scatter(lax.dot_general(cotangent, gated, (((0,), (0,)), ((), ()...  400 us
    scatter-add x1, other arithmetic, block_tables(): kernel[jnp.maximum(distance, 0)]  98.8 us
    gather x1, local copies, waits for them, and re-layouts, block_tables(): kernel[jnp.maximum(distance, 0)]  54.8 us
    psum x1, blocking collectives, per_device(): grad_taps = lax.psum(partial_taps, 'ctx')  40.6 us
    all_gather x1, blocking collectives, per_device(): lax.all_gather(grad_rate_local, 'ctx', axis=1, tiled=True)  32.6 us
    all_gather x1, blocking collectives, per_device(): lax.all_gather(grad_res_local, 'ctx', axis=1, tiled=True)  32 us
    dot_general x3, matrix products, long_conv(): jnp.einsum('ijc,bjc->bic', toeplitz, blocks, precision=lax.Precision.HIGH...  23.2 us
    select_n x2, local copies, waits for them, and re-layouts, block_tables(): jnp.where((distance >= 0)[:, :, None], kernel[jnp.maximum(distance, 0)],...  18.6 us
  transfers between devices with their start and end apart: 7, of which 3 were waited for; matrix products, arithmetic and copies ran while one was open for 7% of the time, Pallas kernels for 0%

commit v1 on v0

--- a/solution.py
+++ b/solution.py
@@ -2,6 +2,13 @@
 import jax.numpy as jnp
 from jax import lax
 from jax.sharding import PartitionSpec as P
+
+
+def refer_digits_on(row_data, at_axis):
+    row_data = jnp.moveaxis(row_data, 0, at_axis)
+    y2 = row_data.shape
+    built = row_data.reshape(*y2[:at_axis], y2[at_axis] * y2[at_axis + 1], *y2[at_axis + 2 :])
+    return built
 
 
 def shifted(value, axis, steps):
@@ -93,9 +100,21 @@
         to_channels(grad_conv).astype(jnp.float32)
     )
     grad_product = to_tokens(grad_prod_chan.astype(jnp.bfloat16)).astype(jnp.float32)
+
+    def pack_the_spots(inputs, mesh_ax, axis_k):
+        nodes = jax.lax.axis_size(mesh_ax)
+        frames = [(dev_i, (dev_i + 1) % nodes) for dev_i in range(nodes)]
+        queue = [inputs]
+        while len(queue) < nodes:
+            queue.append(jax.lax.ppermute(queue[-1], mesh_ax, frames))
+        after = jax.lax.axis_index(mesh_ax)
+        queue = jnp.stack(queue, 0)[(after - jnp.arange(nodes)) % nodes]
+        work_now = refer_digits_on(queue, axis_k)
+        return work_now
+
     grad_residues, grad_log_rate = (
         lax.all_gather(grad_res_local, "ctx", axis=1, tiled=True),
-        lax.all_gather(grad_rate_local, "ctx", axis=1, tiled=True),
+        pack_the_spots(grad_rate_local, "ctx", 1),
     )
     grad_short = jnp.stack(
         [grad_gated * convolved, grad_product * shortened[:, 2], grad_product * shortened[:, 1]],

time: 888 us -> 888 us (level)
  blocking collectives: 117 us -> 80.9 us
  waiting for transfers between devices: 409 us -> 429 us
  local copies, waits for them, and re-layouts: 116 us -> 125 us
    ppermute x0 -> x7, waiting for transfers between devices: none -> 44.5 us  [pack_the_spots(): queue.append(jax.lax.ppermute(queue[-1], mesh_ax, frames))]
    all_gather x1 -> x0, blocking collectives: 32.6 us -> none  [per_device(): lax.all_gather(grad_rate_local, 'ctx', axis=1, tiled=True)]
    reduce_scatter x1, waiting for transfers between devices: 400 us -> 372 us  [per_device(): lax.psum_scatter(lax.dot_general(cotangent, gated, (((0,), (0,)), ((), ()...]
  transfers between devices with their start and end apart: 7 -> 14, of which waited for: 3 -> 10; matrix products, arithmetic and copies ran while one was open for 7% -> 8% of each run, Pallas kernels for 0% -> 0%
where the time goes in v1:
time: 888 us; the launch traced here: 880 us
  waiting for transfers between devices  429 us (48%)
  other arithmetic  133 us (15%)
  local copies, waits for them, and re-layouts  125 us (14%)
  blocking collectives  80.9 us (9%)
  matrix products  72.9 us (8%)
  starting transfers between devices  24 us (3%)
  between operations  14.8 us (2%)
    reduce_scatter x1, waiting for transfers between devices, per_device(): lax.psum_scatter(lax.dot_general(cotangent, gated, (((0,), (0,)), ((), ()...  372 us
    scatter-add x1, other arithmetic, block_tables(): kernel[jnp.maximum(distance, 0)]  98.8 us
    gather x1, local copies, waits for them, and re-layouts, block_tables(): kernel[jnp.maximum(distance, 0)]  54.4 us
    ppermute x7, waiting for transfers between devices, pack_the_spots(): queue.append(jax.lax.ppermute(queue[-1], mesh_ax, frames))  44.5 us
    psum x1, blocking collectives, per_device(): grad_taps = lax.psum(partial_taps, 'ctx')  36.6 us
    all_gather x1, blocking collectives, per_device(): lax.all_gather(grad_res_local, 'ctx', axis=1, tiled=True)  32.2 us
    dot_general x3, matrix products, long_conv(): jnp.einsum('ijc,bjc->bic', toeplitz, blocks, precision=lax.Precision.HIGH...  23.3 us
    select_n x2, local copies, waits for them, and re-layouts, block_tables(): jnp.where((distance >= 0)[:, :, None], kernel[jnp.maximum(distance, 0)],...  18.6 us
  transfers between devices with their start and end apart: 14, of which 10 were waited for; matrix products, arithmetic and copies ran while one was open for 8% of the time, Pallas kernels for 0%

profile of v1, /device:TPU:0, one launch (start us, length us, event | category | flops | bytes accessed | tf_op | source)
XLA Modules:
  0.0 879.6 jit_solution(17515328480070486467)
XLA Ops:
  20.8 5.2 all-to-all-start
  28.1 6.5 all-to-all-done
  38.7 13.0 %multiply_convert_fusion.1 = (bf16[128,1024]{1,0:T(8,128)(2,1)}, f32[128,1024]{1,0:T(8,128)}) fusion(f32[128,3,1024]{2,0,1:T(8,128)S(1)} %multiply_add_fusion, bf16[128,8192]{1,0:T(8,128)(2,1)} %all-gather.2.cloned.1.call-done, bf16[1024,8192]{1,0:T(8,128)(2,1)} %param.10), kind=kOutput, calls=%fused_computation.44 | convolution fusion | flops 2147745792 | bytes 20185088 | tf_op jit(solution)/shard_map/dot_general | solution.py:95
  80.4 5.6 select_bitcast_fusion
  86.0 9.3 %copy.211 = f32[128,128,128]{2,1,0:T(8,128)} copy(f32[128,128,128]{1,0,2:T(8,128)} %select_bitcast_fusion) | data formatting | bytes 16777216 | tf_op jit(solution)/shard_map/transpose(jvp(jit(_where)))/select_n | solution.py:30
  95.3 98.8 %scatter_custom_fusion = f32[128,128]{1,0:T(8,128)S(1)} fusion(s32[16384]{0:T(1024)} %maximum_bitcast_fusion, f32[16384,128]{1,0:T(8,128)} %bitcast.107, f32[]{:T(128)} %constant.20.clone.1), kind=kCustom, calls=%fused_computation.87 | custom fusion | flops 2097152 | bytes 66048 | tf_op jit(solution)/shard_map/transpose(jvp())/scatter-add | solution.py:30
  200.4 54.4 %gather_fusion = f32[16384,128]{1,0:T(8,128)} fusion(f32[128,128]{1,0:T(8,128)S(1)} %copy.179, s32[16384]{0:T(1024)S(1)} %broadcast_clamp_fusion), kind=kCustom, calls=%fused_computation | custom fusion | bytes 16842752 | tf_op jit(solution)/shard_map/jvp()/gather | solution.py:30
  254.8 9.9 %broadcast_select_fusion = f32[128,128,128]{2,1,0:T(8,128)} fusion(f32[128,128,128]{2,1,0:T(8,128)} %bitcast.106, pred[128,128]{1,0:T(8,128)(4,1)} %subtract_compare_fusion), kind=kLoop, calls=%fused_computation.5 | loop fusion | flops 2097152 | bytes 16793600 | tf_op jit(solution)/shard_map/jvp(jit(_where))/select_n | solution.py:30
  264.7 9.3 %copy.181 = f32[128,128,128]{1,0,2:T(8,128)} copy(f32[128,128,128]{2,1,0:T(8,128)} %broadcast_select_fusion) | data formatting | bytes 16777216 | tf_op jit(solution)/shard_map/jvp(jit(_where))/select_n | solution.py:30
  274.0 10.1 %fusion.9 = bf16[8,128,128]{1,0,2:T(8,128)(2,1)S(1)} fusion(f32[128,8,128]{2,1,0:T(8,128)} %fusion.13, f32[128,128,128]{1,0,2:T(8,128)} %copy.181, bf16[128,8,128]{0,2,1:T(8,128)(2,1)} %all-to-all-done), kind=kOutput, calls=%fused_computation.27 | convolution fusion | flops 201588736 | bytes 9437184 | tf_op jit(solution)/shard_map/jvp(ijc,bjc->bic)/dot_general | solution.py:48
  284.2 12.0 %all_to_all.43 = bf16[8,128,128]{1,2,0:T(8,128)(2,1)S(1)} all-to-all(bf16[8,128,128]{1,2,0:T(8,128)(2,1)S(1)} %copy.185), channel_id=1, replica_groups=mesh['ctx'=8,'tp'=4] {'ctx'}, dimensions={0} | all-to-all | bytes 524288 | tf_op jit(solution)/shard_map/all_to_all | solution.py:62
  299.0 17.4 %convolution_bitcast_fusion = f32[8192,1024]{0,1:T(8,128)} fusion(bf16[128,8192]{1,0:T(8,128)(2,1)} %all-gather.2.cloned.1.call-done, f32[128,1024]{1,0:T(8,128)} %copy.208, f32[128,3,1024]{2,0,1:T(8,128)S(1)} %multiply_add_fusion), kind=kOutput, calls=%fused_computation.3 | convolution fusion | flops 2147745792 | bytes 36700160 | tf_op jit(solution)/shard_map/dot_general | solution.py:88
  352.1 7.6 fusion.8
  359.7 32.2 %all_gather.7 = f32[16,1024]{1,0:T(8,128)S(1)} all-gather(f32[16,128]{1,0:T(8,128)S(1)} %fusion.48), channel_id=1, replica_groups=mesh['ctx'=8,'tp'=4] {'ctx'}, dimensions={1}, use_global_device_ids=true | all-gather | bytes 73728 | tf_op jit(solution)/shard_map/all_gather | solution.py:116
  392.7 5.0 all-to-all-start.3
  399.8 11.2 %collective-permute-done.3 = f32[16,128]{1,0:T(8,128)S(1)} collective-permute-done((f32[16,128]{1,0:T(8,128)S(1)}, f32[16,128]{1,0:T(8,128)S(1)}, u32[]{:S(2)}, u32[]{:S(2)}) %collective-permute-start.3) | collective-permute-done | bytes 8224 | tf_op jit(solution)/shard_map/ppermute | solution.py:109
  411.0 6.8 collective-permute-done.4
  417.8 6.7 collective-permute-done.5
  424.5 6.7 collective-permute-done.6
  431.1 6.6 collective-permute-done.7
  437.8 6.5 collective-permute-done.8
  458.5 36.6 %psum.7 = f32[3,3,1024]{2,1,0:T(4,128)} all-reduce(f32[3,3,1024]{2,1,0:T(4,128)S(1)} %pad_maximum_fusion.2), channel_id=1, replica_groups=mesh['ctx'=8,'tp'=4] {'ctx'}, use_global_device_ids=true, to_apply=%region_4.5 | all-reduce | flops 9216 | bytes 73728 | tf_op jit(solution)/shard_map/psum | solution.py:137
  495.1 371.5 %reduce-scatter.2.cloned.1.call-done = f32[1024,1024]{0,1:T(8,128)} async-done(((f32[8192,1024]{0,1:T(8,128)}), f32[1024,1024]{0,1:T(8,128)}) %reduce-scatter.2.cloned.1.call-update) | async-done | bytes 4194320 | tf_op jit(solution)/shard_map/reduce_scatter | solution.py:87
  866.6 5.3 copy.206
  (155 shorter events, 110.5 us)
Async XLA Ops:
  7.2 31.6 %all-gather.2.cloned.1.call-start = ((), (), s32[]{:S(2)}) async-start(), calls=%async_computation.5 | async-start | bytes 2621440 | tf_op jit(solution)/shard_map/all_gather | solution.py:86
  8.7 7.7 collective-permute-start
  13.6 21.0 %copy-start.16 = (f32[128]{0:T(128)}, f32[128]{0:T(128)S(1)}, u32[]{:S(2)}) copy-start(f32[128]{0:T(128)S(1)} %broadcast_subtract_fusion) | copy-start | bytes 1540
  15.0 23.7 %copy-start.13 = (f32[16,128]{1,0:T(8,128)}, f32[16,128]{1,0:T(8,128)S(1)}, u32[]{:S(2)}) copy-start(f32[16,128]{1,0:T(8,128)S(1)} %get-tuple-element.58) | copy-start | bytes 24580
  15.8 2.5 copy-start.3
  15.8 2.5 copy-start.5
  15.8 2.5 copy-start.7
  20.8 13.8 %all-to-all-start = ((bf16[128,8,128]{0,2,1:T(8,128)(2,1)}), bf16[128,8,128]{0,2,1:T(8,128)(2,1)}, u32[]{:S(2)}, u32[]{:S(2)}) async-start(bf16[128,8,128]{0,2,1:T(8,128)(2,1)} %bitcast.111), calls=%async_computation | async-start | bytes 524288 | tf_op jit(solution)/shard_map/all_to_all | solution.py:58
  38.7 19.2 %copy-start.14 = (f32[2,16,128]{2,1,0:T(8,128)}, f32[2,16,128]{2,1,0:T(8,128)S(1)}, u32[]{:S(2)}) copy-start(f32[2,16,128]{2,1,0:T(8,128)S(1)} %slice_add_fusion.3) | copy-start | bytes 49156
  53.5 12.3 %all-to-all-start.2 = ((bf16[128,8,128]{0,2,1:T(8,128)(2,1)}), bf16[128,8,128]{0,2,1:T(8,128)(2,1)}, u32[]{:S(2)}, u32[]{:S(2)}) async-start(bf16[128,8,128]{0,2,1:T(8,128)(2,1)} %bitcast.110), calls=%async_computation.2 | async-start | bytes 524288 | tf_op jit(solution)/shard_map/all_to_all | solution.py:58
  57.5 809.1 %reduce-scatter.2.cloned.1.call-start = ((), (), s32[]{:S(2)}) async-start(), calls=%async_computation.6 | async-start | bytes 37748736 | tf_op jit(solution)/shard_map/reduce_scatter | solution.py:87
  77.1 3.3 copy-start.2
  348.2 49.6 %collective-permute-start.2 = (f32[16,128]{1,0:T(8,128)S(1)}, f32[16,128]{1,0:T(8,128)S(1)}, u32[]{:S(2)}, u32[]{:S(2)}) collective-permute-start(f32[16,128]{1,0:T(8,128)S(1)} %get-tuple-element.52), channel_id=1, source_target_pairs={{0,4},{4,8},{8,12},{12,16},{16,20},{20,24},{24,28},{28,0},{1,5},{5... | collective-permute-start | bytes 24584 | tf_op jit(solution)/shard_map/ppermute | solution.py:109
  392.7 52.2 %all-to-all-start.3 = ((bf16[8,128,128]{1,2,0:T(8,128)(2,1)}), bf16[8,128,128]{1,2,0:T(8,128)(2,1)}, u32[]{:S(2)}, u32[]{:S(2)}) async-start(bf16[8,128,128]{1,2,0:T(8,128)(2,1)} %copy.192), calls=%async_computation.3 | async-start | bytes 524288 | tf_op jit(solution)/shard_map/all_to_all | solution.py:62
  397.8 13.2 %collective-permute-start.3 = (f32[16,128]{1,0:T(8,128)S(1)}, f32[16,128]{1,0:T(8,128)S(1)}, u32[]{:S(2)}, u32[]{:S(2)}) collective-permute-start(f32[16,128]{1,0:T(8,128)S(1)} %collective-permute-done.2), channel_id=1, source_target_pairs={{0,4},{4,8},{8,12},{12,16},{16,20},{20,24},{24,28},{28,0},{1,5},{5... | collective-permute-start | bytes 24584 | tf_op jit(solution)/shard_map/ppermute | solution.py:109
  411.0 6.8 collective-permute-start.4
  417.8 6.7 collective-permute-start.5
  424.4 6.7 collective-permute-start.6
  431.1 6.7 collective-permute-start.7
  437.8 6.5 collective-permute-start.8
  450.4 6.1 copy-start.4
  450.4 6.1 copy-start.6
  450.4 6.1 copy-start.8
  450.4 5.9 collective-permute-start.1
  (7 other events, 10.5 us)
Sparse Core Ops, SparseCore 0:
  9.6 25.2 all-gather.1
  316.6 549.9 reduce-scatter.1
